TPU v7x, 128 devices: a whole 4x4x4 slice. The times are simulated.
128 devices in a mesh: section: 8 (over z, x_lo), tensor: 16 (over x_hi, y, core).
Axes of the slice: x: 4 (x_hi: 2, x_lo: 2; x = x_hi * 2 + x_lo), y: 4, z: 4, core: 2. Of those that a mesh axis runs over, the one named last changes fastest.
Arguments:
- state: bfloat16 [8, 2048, 5120], P('section', 'tensor'), may hold values from -6 to 6
- docs: int32 [8, 2048], P('section', 'tensor'), may hold values from 0 to 15, never falling along the last dimension, each value on 1 to 512 neighbouring positions
- gain: float32 [8, 5120], P('section'), may hold values from 0.25 to 1.75
- w_query: bfloat16 [8, 5120, 4096], P('section', None, 'tensor'), may hold values from -1 to 1
- w_keyval: bfloat16 [8, 5120, 2048], P('section', None, 'tensor'), may hold values from -1 to 1
- w_out: bfloat16 [8, 4096, 5120], P('section', 'tensor'), may hold values from -0.09375 to 0.09375
Outputs:
- next_state: bfloat16 [8, 2048, 5120], P('section', 'tensor')
- next_docs: int32 [8, 2048], P('section', 'tensor')
Inputs may be any that keep to these rules, and one draw needn't show every extreme that they name: `docs`: in each layer's row the ids never fall; each document holds 1 to 512 tokens and one holds exactly 512.
All inputs are finite; a program needn't handle non-finite values.
Results may differ from a plain program's by a relative error of at most 0.014.
Values may be sent and summed in bfloat16 or wider, within the bound.
A program may use at most 128 MiB of HBM per device.

v0:
```python
import jax
import jax.numpy as jnp
from jax import lax
from jax.sharding import PartitionSpec as P


def partner(value, axis, apart):
    return lax.ppermute(value, axis, [(i, i ^ 1 << apart) for i in range(lax.axis_size(axis))])


def shifted(value, axis, by):
    size = lax.axis_size(axis)
    return lax.ppermute(value, axis, [(i, (i + by) % size) for i in range(size)])


def norm_tokens(values_in, gain_row):
    widened = values_in.astype(jnp.float32)
    factor = lax.rsqrt(jnp.mean(widened * widened, axis=-1, keepdims=True) + 1e-05)
    return (widened * factor * gain_row).astype(jnp.bfloat16)


def attend(query_rows, key_rows, value_rows, doc_ids, first_row):
    count = query_rows.shape[0]
    length = key_rows.shape[0]
    scores = jnp.dot(query_rows, key_rows.T, preferred_element_type=jnp.float32) * key_rows.shape[
        1
    ] ** (-0.5)
    row_pos = first_row + lax.iota(jnp.int32, count)
    col_pos = lax.iota(jnp.int32, length)
    query_docs = lax.dynamic_slice_in_dim(doc_ids, first_row, count, 0)
    visible = (col_pos[None, :] <= row_pos[:, None]) & (
        doc_ids[None, :length] == query_docs[:, None]
    )
    scores = jnp.where(visible, scores, -jnp.inf)
    highest = jnp.max(scores, axis=-1, keepdims=True)
    expo = jnp.exp(scores - highest)
    probs = (expo / jnp.sum(expo, axis=-1, keepdims=True)).astype(jnp.bfloat16)
    return jnp.dot(probs, value_rows, preferred_element_type=jnp.float32).astype(jnp.bfloat16)


def local(state, docs, gain, w_query, w_keyval, w_out):
    local_state = state[0]
    normed = norm_tokens(local_state, gain[0])
    everyone, all_docs = (
        lax.all_gather(normed, "tensor", axis=0, tiled=True),
        lax.all_gather(docs[0], "tensor", axis=0, tiled=True),
    )
    total_rows = everyone.shape[0]
    query = jnp.dot(everyone, w_query[0], preferred_element_type=jnp.float32).astype(jnp.bfloat16)
    own_half = jnp.dot(everyone, w_keyval[0], preferred_element_type=jnp.float32).astype(
        jnp.bfloat16
    )
    other_half = partner(own_half, "tensor", 0)
    is_odd = lax.axis_index("tensor") % 2 == 1
    key_rows = jnp.where(is_odd, other_half, own_half)
    value_rows = jnp.where(is_odd, own_half, other_half)
    head_size = key_rows.shape[1]
    heads_here = query.shape[1] // head_size
    block_size = min(512, total_rows)
    block_count = total_rows // block_size

    def block_out(block_index):
        first_row = block_index * block_size
        block_rows = lax.dynamic_slice_in_dim(query, first_row, block_size, 0)
        return jnp.concatenate(
            [
                attend(
                    block_rows[:, head_index * head_size : (head_index + 1) * head_size],
                    key_rows,
                    value_rows,
                    all_docs,
                    first_row,
                )
                for head_index in range(heads_here)
            ],
            axis=1,
        )

    attended = lax.map(block_out, jnp.arange(block_count, dtype=jnp.int32)).reshape(
        total_rows, query.shape[1]
    )
    delta = lax.psum_scatter(
        jnp.dot(attended, w_out[0], preferred_element_type=jnp.float32).astype(jnp.bfloat16),
        "tensor",
        scatter_dimension=0,
        tiled=True,
    ).astype(jnp.float32)
    layer_out = (local_state.astype(jnp.float32) + delta).astype(jnp.bfloat16)
    moved_state, moved_docs = shifted((layer_out[None], docs), "section", 1)
    return (moved_state, moved_docs)


def solution(mesh):
    in_specs = (
        P("section", "tensor", None),
        P("section", "tensor"),
        P("section", None),
        P("section", None, "tensor"),
        P("section", None, "tensor"),
        P("section", "tensor", None),
    )
    out_specs = (P("section", "tensor", None), P("section", "tensor"))
    return jax.shard_map(local, mesh=mesh, in_specs=in_specs, out_specs=out_specs, check_vma=False)
```

profile of v0, /device:TPU:0, one launch (start us, length us, event | category | flops | bytes accessed | tf_op | source)
XLA Modules:
  0.0 437.7 jit_solution(933294676095883905)
XLA Ops:
  7.2 1.8 fusion.10
  9.0 2.8 fusion.12
  11.9 24.4 %all-gather = s32[1,2048]{1,0:T(1,128)S(1)} all-gather(s32[1,128]{1,0:T(1,128)S(1)} %copy-done.1), channel_id=2, replica_groups=mesh['section'=8,'tensor'=16] {'tensor'}, dimensions={1}, use_global_device_ids=true | all-gather | bytes 8704 | tf_op jit(solution)/shard_map/all_gather | solution.py:46
  36.3 106.5 %all-gather.3.cloned.1.call-done = bf16[2048,5120]{1,0:T(8,128)(2,1)} async-done(((bf16[128,5120]{1,0:T(8,128)(2,1)}), bf16[2048,5120]{1,0:T(8,128)(2,1)}) %all-gather.3.cloned.1.call-update) | async-done | bytes 20971536 | tf_op jit(solution)/shard_map/all_gather | solution.py:45
  142.8 12.4 %convolution_convert_fusion.1 = bf16[2048,128]{1,0:T(8,128)(2,1)S(1)} fusion(bf16[2048,5120]{1,0:T(8,128)(2,1)} %all-gather.3.cloned.1.call-done, bf16[1,5120,128]{2,1,0:T(8,128)(2,1)} %param.12), kind=kOutput, calls=%fused_computation.32 | convolution fusion | flops 2684616704 | bytes 22806528 | tf_op jit(solution)/shard_map/dot_general | solution.py:50
  156.1 8.9 %fusion.17 = bf16[2048,256]{1,0:T(8,128)(2,1)} fusion(bf16[2048,5120]{1,0:T(8,128)(2,1)S(1)} %copy-done.2, bf16[1,5120,256]{2,1,0:T(8,128)(2,1)} %param.11), kind=kOutput, calls=%fused_computation.31 | convolution fusion | flops 5369233408 | bytes 24641536 | tf_op jit(solution)/shard_map/dot_general | solution.py:49
  165.0 1.1 broadcast_select_fusion
  166.1 51.3 %while.10 = (s32[]{:T(128)}, bf16[4,512,256]{2,1,0:T(8,128)(2,1)}, s32[4]{0:T(128)S(1)}, s32[2048]{0:T(1024)S(1)}, bf16[2048,256]{1,0:T(8,128)(2,1)}, /*index=5*...) while((s32[]{:T(128)}, bf16[4,512,256]{2,1,0:T(8,128)(2,1)}, ...), condition=%wide.region_6.7_spmd, body=%wide.region_1.6_spmd.sunk | while | flops 1097464320 | bytes 29412048 | solution.py:79
  166.1 0.7 dynamic_slice.13
  167.5 2.3 fusion.48
  169.9 0.7 fusion.49
  170.6 2.2 fusion.50
  172.8 2.4 fusion.45
  175.1 0.7 fusion.46
  175.8 2.2 fusion.47
  178.2 0.7 constant_dynamic-update-slice_fusion.2
  178.9 0.7 dynamic_slice.13
  180.3 2.4 fusion.48
  182.7 0.7 fusion.49
  183.4 2.2 fusion.50
  185.6 2.4 fusion.45
  187.9 0.7 fusion.46
  188.7 2.2 fusion.47
  191.0 0.7 constant_dynamic-update-slice_fusion.2
  191.7 0.7 dynamic_slice.13
  193.2 2.3 fusion.48
  195.5 0.7 fusion.49
  196.2 2.2 fusion.50
  198.4 2.4 fusion.45
  200.8 0.7 fusion.46
  201.5 2.2 fusion.47
  203.8 0.7 constant_dynamic-update-slice_fusion.2
  204.5 0.7 dynamic_slice.13
  206.0 2.4 fusion.48
  208.3 0.7 fusion.49
  209.1 2.2 fusion.50
  211.2 2.4 fusion.45
  213.6 0.7 fusion.46
  214.3 2.2 fusion.47
  216.6 0.7 constant_dynamic-update-slice_fusion.2
  217.4 11.2 %convolution_convert_fusion = bf16[2048,5120]{1,0:T(8,128)(2,1)} fusion(bf16[2048,256]{1,0:T(8,128)(2,1)} %bitcast.43, bf16[1,256,5120]{2,1,0:T(8,128)(2,1)S(1)} %copy-done), kind=kOutput, calls=%fused_computation.20 | convolution fusion | flops 5379194880 | bytes 24641536 | tf_op jit(solution)/shard_map/dot_general | solution.py:83
  228.7 166.4 %reduce-scatter.2.cloned.1.call-done = bf16[128,5120]{1,0:T(8,128)(2,1)} async-done(((bf16[2048,5120]{1,0:T(8,128)(2,1)}), bf16[128,5120]{1,0:T(8,128)(2,1)}) %reduce-scatter.2.cloned.1.call-update) | async-done | bytes 1310736 | tf_op jit(solution)/shard_map/reduce_scatter | solution.py:82
  395.0 2.0 fusion.20
  397.1 0.6 collective-permute-start.1
  397.7 2.5 collective-permute-start.2
  400.1 29.1 %collective-permute-done.2 = s32[1,128]{1,0:T(1,128)S(1)} collective-permute-done((s32[1,128]{1,0:T(1,128)S(1)}, s32[1,128]{1,0:T(1,128)S(1)}, u32[]{:S(2)}, u32[]{:S(2)}) %collective-permute-start.2) | collective-permute-done | bytes 544 | tf_op jit(solution)/shard_map/ppermute | solution.py:13
  429.3 1.1 copy.22
  430.3 0.5 copy.23
  (32 shorter events, 1.9 us)
Async XLA Ops:
  7.2 210.2 %copy-start = (bf16[1,256,5120]{2,1,0:T(8,128)(2,1)S(1)}, bf16[1,256,5120]{2,1,0:T(8,128)(2,1)}, u32[]{:S(2)}) copy-start(bf16[1,256,5120]{2,1,0:T(8,128)(2,1)} %param.13) | copy-start | bytes 7864324
  7.2 4.7 %copy-start.1 = (s32[1,128]{1,0:T(1,128)S(1)}, s32[1,128]{1,0:T(1,128)}, u32[]{:S(2)}) copy-start(s32[1,128]{1,0:T(1,128)} %param.9) | copy-start | bytes 1540
  7.2 135.6 %all-gather.3.cloned.1.call-start = ((), (), s32[]{:S(2)}) async-start(), calls=%async_computation.1 | async-start | bytes 22282240 | tf_op jit(solution)/shard_map/all_gather | solution.py:45
  11.8 383.2 %reduce-scatter.2.cloned.1.call-start = ((), (), s32[]{:S(2)}) async-start(), calls=%async_computation.2 | async-start | bytes 22282240 | tf_op jit(solution)/shard_map/reduce_scatter | solution.py:82
  142.8 13.3 %copy-start.2 = (bf16[2048,5120]{1,0:T(8,128)(2,1)S(1)}, bf16[2048,5120]{1,0:T(8,128)(2,1)}, u32[]{:S(2)}) copy-start(bf16[2048,5120]{1,0:T(8,128)(2,1)} %all-gather.3.cloned.1.call-done) | copy-start | bytes 62914564
  155.2 9.8 %collective-permute-start = (bf16[2048,128]{1,0:T(8,128)(2,1)S(1)}, bf16[2048,128]{1,0:T(8,128)(2,1)S(1)}, u32[]{:S(2)}, u32[]{:S(2)}) collective-permute-start(bf16[2048,128]{1,0:T(8,128)(2,1)S(1)} %convolution_convert_fusion.1), channel_id=1, source_target_pairs={{0,1},{1,0},{2,3},{3,2},{4,5},{5,4},{6,7},{7,6},{8,9},{9,8},{10,11... | collective-permute-start | bytes 1572872 | tf_op jit(solution)/shard_map/ppermute | solution.py:8
  397.1 32.2 %collective-permute-start.1 = (bf16[1,128,5120]{2,1,0:T(8,128)(2,1)S(1)}, bf16[1,128,5120]{2,1,0:T(8,128)(2,1)S(1)}, u32[]{:S(2)}, u32[]{:S(2)}) collective-permute-start(bf16[1,128,5120]{2,1,0:T(8,128)(2,1)S(1)} %fusion.20), channel_id=1, source_target_pairs={{0,16},{16,32},{32,48},{48,64},{64,80},{80,96},{96,112},{112,0},{1... | collective-permute-start | bytes 3932168 | tf_op jit(solution)/shard_map/ppermute | solution.py:13
  397.7 31.6 %collective-permute-start.2 = (s32[1,128]{1,0:T(1,128)S(1)}, s32[1,128]{1,0:T(1,128)S(1)}, u32[]{:S(2)}, u32[]{:S(2)}) collective-permute-start(s32[1,128]{1,0:T(1,128)S(1)} %copy-done.1), channel_id=1, source_target_pairs={{0,16},{16,32},{32,48},{48,64},{64,80},{80,96},{96,112},{112,0},{1... | collective-permute-start | bytes 1544 | tf_op jit(solution)/shard_map/ppermute | solution.py:13
Sparse Core Ops, SparseCore 0:
  12.0 130.7 all-gather.2
  228.8 166.2 reduce-scatter.1
where the time goes:
time: 439 us; the launch traced here: 438 us
  waiting for transfers between devices  302 us (69%)
  matrix products  68.8 us (16%)
  blocking collectives  24.4 us (6%)
  between operations  14.1 us (3%)
  other arithmetic  13.4 us (3%)
  local copies, waits for them, and re-layouts  8.47 us (2%)
    reduce_scatter x1, waiting for transfers between devices, local(): lax.psum_scatter(jnp.dot(attended, w_out[0], preferred_element_type=jnp.f...  166 us
    all_gather x1, waiting for transfers between devices, local(): lax.all_gather(normed, 'tensor', axis=0, tiled=True)  106 us
    ppermute x2, waiting for transfers between devices, shifted(): lax.ppermute(value, axis, [(i, (i + by) % size) for i in range(size)])  29.1 us
    all_gather x1, blocking collectives, local(): lax.all_gather(docs[0], 'tensor', axis=0, tiled=True)  24.4 us
    dot_general x8, matrix products, attend(): jnp.dot(query_rows, key_rows.T, preferred_element_type=jnp.float32)  18.8 us
    dot_general x8, matrix products, attend(): jnp.dot(probs, value_rows, preferred_element_type=jnp.float32)  17.3 us
    dot_general x1, matrix products, local(): jnp.dot(everyone, w_keyval[0], preferred_element_type=jnp.float32)  12.4 us
    dot_general x1, matrix products, local(): jnp.dot(attended, w_out[0], preferred_element_type=jnp.float32)  11.2 us
  transfers between devices with their start and end apart: 5, of which 3 were waited for; matrix products, arithmetic and copies ran while one was open for 2% of the time, Pallas kernels for 0%

commit v1 on v0

v1 whole, which is shorter than its diff:
```python
import functools

import jax
import jax.numpy as jnp
from jax import lax
from jax.experimental import pallas as pl
from jax.experimental.pallas import tpu as pltpu
from jax.sharding import PartitionSpec as P

MESH = pl.DeviceIdType.MESH
BLK = 128
HALF = 64
HD = 128
WIN = 5
PAD = WIN - 1
YS = 4
NJ = 10
NW = 5
SLOTS = ((0, 0), (1, 0), (0, 3), (0, 1), (1, 3), (1, 1), (0, 2), (1, 2))
OWN, ACROSS, BEHIND, AHEAD, BEHIND2, AHEAD2, FAR, FAR2 = range(8)
LOG2E = 1.4426950408889634
FIRST = pl.ds(0, HALF)
SECOND = pl.ds(HALF, HALF)


def body(
    state_ref, docs_ref, gain_ref, wq_ref, wkv_ref, wo_ref,
    out_ref, odocs_ref,
    state, gain, xg, w, wo, q, kv, dc, att, att_out,
    far, fwd, bwd, mine, half_f, half_b, got_f, got_b, done,
    load_sem, xs_sem, xr_sem, dsend, drecv, ws_sem, wr_sem, kvs_sem, kvr_sem,
    wos_sem, wor_sem, ats_sem, atr_sem, rs_send, rs_recv, sh_send, sh_recv,
):
    width = state.shape[1]
    cw = width // NJ
    ww = width // NW
    sec = lax.axis_index("section")
    ten = lax.axis_index("tensor")
    nsec = lax.axis_size("section")
    xh, y, core = ten // (2 * YS), (ten // 2) % YS, ten % 2

    def at(dh, dy, dcore=0):
        return (sec, ((xh + dh) % 2) * (2 * YS) + ((y + dy) % YS) * 2 + (core + dcore) % 2)

    def block_of(dh, dy):
        return ((xh + dh) % 2) * YS + (y + dy) % YS

    twin, across, ahead, behind = at(0, 0, 1), at(1, 0), at(0, 1), at(0, 3)
    following = ((sec + 1) % nsec, ten)
    before = ((sec + nsec - 1) % nsec, ten)

    loads = [
        pltpu.make_async_copy(state_ref.at[0], state, load_sem.at[0]),
        pltpu.make_async_copy(gain_ref, gain, load_sem.at[1]),
        pltpu.make_async_copy(docs_ref, dc.at[PAD + 2 * block_of(0, 0) + core], load_sem.at[2]),
        pltpu.make_async_copy(wq_ref.at[0], w.at[core], load_sem.at[3]),
        pltpu.make_async_copy(
            wkv_ref.at[0], w.at[2, :, pl.ds(pl.multiple_of(core * HD, HD), HD)], load_sem.at[4]
        ),
        pltpu.make_async_copy(
            wo_ref.at[0], wo.at[0, pl.ds(pl.multiple_of(core * 256, 256), 256), :], load_sem.at[5]
        ),
    ]
    for copy in loads:
        copy.start()

    barrier = pltpu.get_barrier_semaphore()
    for other in (twin, across, ahead, behind, following, before):
        pl.semaphore_signal(barrier, inc=1, device_id=other, device_id_type=MESH)

    for index in range(PAD):
        kv[index] = jnp.zeros((BLK, 2 * HD), jnp.bfloat16)
        dc[index] = jnp.full((1, BLK), -1, jnp.int32)

    def remote(src, dst, send, recv, target):
        return pltpu.make_async_remote_copy(
            src_ref=src, dst_ref=dst, send_sem=send, recv_sem=recv, device_id=target, device_id_type=MESH
        )

    sent = []

    def go(copy):
        copy.start()
        sent.append(copy)
        return copy

    def piece(number, src, dst, part, target):
        rows = FIRST if part == 0 else SECOND
        return remote(
            xg.at[src, rows, :], xg.at[dst, rows, :], xs_sem.at[number], xr_sem.at[dst, part], target
        )

    def arrived(slot, part):
        rows = FIRST if part == 0 else SECOND
        remote(
            xg.at[slot, rows, :], xg.at[slot, rows, :], xs_sem.at[0], xr_sem.at[slot, part], twin
        ).wait_recv()

    def doc_pair(dh, dy):
        return dc.at[pl.ds(PAD + 2 * block_of(dh, dy), 2)]

    def send_docs(number, dh, dy, recv, target):
        ref = doc_pair(dh, dy)
        return remote(ref, ref, dsend.at[number], drecv.at[recv], target)

    def docs_arrived(recv, dh, dy):
        ref = doc_pair(dh, dy)
        remote(ref, ref, dsend.at[0], drecv.at[recv], twin).wait_recv()

    loads[0].wait()
    loads[1].wait()

    def norm(rows):
        wide = state[rows, :].astype(jnp.float32)
        factor = lax.rsqrt(jnp.mean(wide * wide, axis=-1, keepdims=True) + 1e-05)
        xg[OWN, rows, :] = (wide * factor * gain[...]).astype(jnp.bfloat16)

    norm(FIRST)
    pl.semaphore_wait(barrier, 6)
    go(piece(0, OWN, BEHIND, 0, ahead))
    go(piece(1, OWN, ACROSS, 0, across))
    norm(SECOND)
    go(piece(2, OWN, AHEAD, 1, behind))
    go(piece(3, OWN, BEHIND, 1, ahead))
    go(piece(4, OWN, AHEAD, 0, behind))
    across_last = piece(5, OWN, ACROSS, 1, across)
    across_last.start()

    loads[2].wait()
    own_docs = dc.at[PAD + 2 * block_of(0, 0) + core]
    go(remote(own_docs, own_docs, dsend.at[0], drecv.at[0], twin))
    go(remote(docs_ref, odocs_ref, dsend.at[9], drecv.at[9], following))
    go(remote(wq_ref.at[0], w.at[core], ws_sem.at[0], wr_sem.at[0], twin))
    kv_cols = w.at[2, :, pl.ds(pl.multiple_of(core * HD, HD), HD)]
    go(remote(wkv_ref.at[0], kv_cols, ws_sem.at[1], wr_sem.at[1], twin))
    twin_docs = dc.at[PAD + 2 * block_of(0, 0) + 1 - core]
    remote(twin_docs, twin_docs, dsend.at[0], drecv.at[0], twin).wait_recv()
    go(send_docs(1, 0, 0, 1, across))
    go(send_docs(2, 0, 0, 2, ahead))
    go(send_docs(3, 0, 0, 3, behind))

    def project(slot, count):
        rows = xg[pl.ds(slot, count)].reshape(count * BLK, width)
        for index in range(3):
            res = jnp.dot(rows, w[index], preferred_element_type=jnp.float32).astype(jnp.bfloat16)
            for one in range(count):
                dh, dy = SLOTS[slot + one]
                part = res[one * BLK : (one + 1) * BLK]
                if index < 2:
                    q[dh * YS + dy, 2 * index] = part[:, :HD]
                    q[dh * YS + dy, 2 * index + 1] = part[:, HD:]
                else:
                    kv[PAD + 2 * block_of(dh, dy) + core] = part
        for one in range(count):
            dh, dy = SLOTS[slot + one]
            ref = kv.at[PAD + 2 * block_of(dh, dy) + core]
            go(remote(ref, ref, kvs_sem.at[slot + one], kvr_sem.at[slot + one], twin))

    def wo_piece(chunk):
        return pl.ds(chunk * ww, ww)

    def wo_across(chunk):
        dst = wo.at[1, pl.ds(pl.multiple_of(core * 256, 256), 256), wo_piece(chunk)]
        return remote(wo_ref.at[0, :, wo_piece(chunk)], dst, wos_sem.at[chunk], wor_sem.at[chunk], across)

    def wo_relay(chunk):
        ref = wo.at[1, pl.ds(pl.multiple_of(core * 256, 256), 256), wo_piece(chunk)]
        return remote(ref, ref, wos_sem.at[NW + chunk], wor_sem.at[NW + chunk], twin)

    def pass_wo(chunk):
        wo_across(chunk).wait_recv()
        go(wo_relay(chunk))

    arrived(BEHIND, 0)
    go(piece(6, BEHIND, FAR, 0, ahead))
    arrived(AHEAD, 1)
    go(piece(7, AHEAD, FAR, 1, behind))
    arrived(ACROSS, 0)
    go(piece(8, ACROSS, BEHIND2, 0, ahead))
    go(piece(10, ACROSS, AHEAD2, 0, behind))
    across_last.wait_send()
    for chunk in range(NW):
        go(wo_across(chunk))
    arrived(ACROSS, 1)
    go(piece(9, ACROSS, AHEAD2, 1, behind))
    go(piece(11, ACROSS, BEHIND2, 1, ahead))
    docs_arrived(1, 1, 0)
    go(send_docs(4, 1, 0, 4, ahead))
    go(send_docs(5, 1, 0, 5, behind))
    docs_arrived(2, 0, 3)
    go(send_docs(6, 0, 3, 6, ahead))
    docs_arrived(3, 0, 1)
    go(remote(
        wo_ref.at[0], wo.at[0, pl.ds(pl.multiple_of(core * 256, 256), 256), :],
        wos_sem.at[2 * NW], wor_sem.at[2 * NW], twin,
    ))

    for copy in loads[3:]:
        copy.wait()
    remote(w.at[1 - core], w.at[1 - core], ws_sem.at[0], wr_sem.at[0], twin).wait_recv()
    kv_cols2 = w.at[2, :, pl.ds(pl.multiple_of((1 - core) * HD, HD), HD)]
    remote(kv_cols2, kv_cols2, ws_sem.at[1], wr_sem.at[1], twin).wait_recv()
    project(OWN, 2)
    docs_arrived(4, 1, 3)
    go(send_docs(7, 1, 3, 7, ahead))
    docs_arrived(5, 1, 1)
    arrived(BEHIND, 1)
    arrived(AHEAD, 0)
    project(BEHIND, 2)
    pass_wo(0)
    arrived(BEHIND2, 0)
    go(piece(12, BEHIND2, FAR2, 0, ahead))
    arrived(AHEAD2, 1)
    go(piece(13, AHEAD2, FAR2, 1, behind))
    pass_wo(1)
    arrived(FAR, 0)
    arrived(FAR, 1)
    project(FAR, 1)
    pass_wo(2)
    arrived(BEHIND2, 1)
    arrived(AHEAD2, 0)
    project(BEHIND2, 2)
    docs_arrived(6, 0, 2)
    docs_arrived(7, 1, 2)
    arrived(FAR2, 0)
    arrived(FAR2, 1)
    project(FAR2, 1)
    pass_wo(3)
    for slot in range(8):
        dh, dy = SLOTS[slot]
        ref = kv.at[PAD + 2 * block_of(dh, dy) + 1 - core]
        remote(ref, ref, kvs_sem.at[slot], kvr_sem.at[slot], twin).wait_recv()

    factor = HD ** (-0.5) * LOG2E

    def attend(dh, dy):
        block = 2 * block_of(dh, dy) + core
        heads = q[dh * YS + dy].reshape(4 * BLK, HD)
        keys = kv[pl.ds(block, WIN), :, :HD].reshape(WIN * BLK, HD)
        values = kv[pl.ds(block, WIN), :, HD:].reshape(WIN * BLK, HD)
        scores = lax.dot_general(
            heads, keys, (((1,), (1,)), ((), ())), preferred_element_type=jnp.float32
        ).reshape(4, BLK, WIN * BLK)
        key_docs = dc[pl.ds(block, WIN)].astype(jnp.float32)
        row_docs = jnp.broadcast_to(key_docs[WIN - 1], (BLK, BLK)).T
        tiles = []
        for index in range(WIN):
            same = row_docs == key_docs[index]
            if index == WIN - 1:
                same = same & (
                    lax.broadcasted_iota(jnp.int32, (BLK, BLK), 1)
                    <= lax.broadcasted_iota(jnp.int32, (BLK, BLK), 0)
                )
            tiles.append(
                jnp.where(same[None], scores[:, :, index * BLK : (index + 1) * BLK], -jnp.inf)
            )
        top = functools.reduce(jnp.maximum, tiles)
        top = jnp.max(top, axis=-1, keepdims=True) * factor
        tiles = [jnp.exp2(tile * factor - top) for tile in tiles]
        total = jnp.sum(functools.reduce(jnp.add, tiles), axis=-1, keepdims=True)
        probs = jnp.concatenate([tile.astype(jnp.bfloat16) for tile in tiles], axis=-1)
        res = jnp.dot(
            probs.reshape(4 * BLK, WIN * BLK), values, preferred_element_type=jnp.float32
        ).reshape(4, BLK, HD)
        return (res / total).astype(jnp.bfloat16)

    def att_copy(dy):
        return remote(att_out.at[dy], att.at[1, dy], ats_sem.at[dy], atr_sem.at[dy], across)

    def attend_other(dy, carry):
        res = attend(1, dy)
        for head in range(4):
            att_out[dy, :, head * HD : (head + 1) * HD] = res[head]
        att_copy(dy).start()
        return carry

    def attend_own(dy, carry):
        res = attend(0, dy)
        for head in range(4):
            att[0, dy, :, head * HD : (head + 1) * HD] = res[head]
        return carry

    lax.fori_loop(0, YS, attend_other, 0)
    pass_wo(4)
    lax.fori_loop(0, YS, attend_own, 0)

    own_wo = wo.at[0, pl.ds(pl.multiple_of((1 - core) * 256, 256), 256), :]
    remote(own_wo, own_wo, wos_sem.at[2 * NW], wor_sem.at[2 * NW], twin).wait_recv()
    for dy in range(YS):
        att_copy(dy).wait_recv()

    def half_copies(k):
        return (
            remote(far.at[k, FIRST, :], half_f.at[k], rs_send.at[0, k], rs_recv.at[0, k], ahead),
            remote(far.at[k, SECOND, :], half_b.at[k], rs_send.at[1, k], rs_recv.at[1, k], behind),
        )

    def full_copies(k):
        return (
            remote(fwd.at[k], got_f.at[k], rs_send.at[2, k], rs_recv.at[2, k], ahead),
            remote(bwd.at[k], got_b.at[k], rs_send.at[3, k], rs_recv.at[3, k], behind),
        )

    def cols(k):
        return pl.ds(pl.multiple_of(k * cw, cw), cw)

    def shift_copy(k):
        return remote(done.at[k], out_ref.at[0, :, cols(k)], sh_send.at[k], sh_recv.at[k], following)

    def step(i, carry):
        for chunk in range(NW):
            @pl.when(i == chunk * (NJ // NW))
            def _():
                ref = wo.at[1, pl.ds(pl.multiple_of((1 - core) * 256, 256), 256), wo_piece(chunk)]
                remote(
                    ref, ref, wos_sem.at[NW + chunk], wor_sem.at[NW + chunk], twin
                ).wait_recv()

        @pl.when(i < NJ)
        def _():
            res = jnp.dot(
                att[0].reshape(YS * BLK, 4 * HD), wo[0, :, cols(i)], preferred_element_type=jnp.float32
            ) + jnp.dot(
                att[1].reshape(YS * BLK, 4 * HD), wo[1, :, cols(i)], preferred_element_type=jnp.float32
            )
            far[i] = res[2 * BLK : 3 * BLK].astype(jnp.bfloat16)
            for copy in half_copies(i):
                copy.start()
            mine[i] = res[:BLK]
            fwd[i] = res[BLK : 2 * BLK].astype(jnp.bfloat16)
            bwd[i] = res[3 * BLK :].astype(jnp.bfloat16)

        @pl.when((i >= 1) & (i <= NJ))
        def _():
            k = i - 1
            first, second = half_copies(k)
            to_f, to_b = full_copies(k)
            first.wait_recv()
            fwd[k, FIRST, :] = (
                fwd[k, FIRST, :].astype(jnp.float32) + half_f[k].astype(jnp.float32)
            ).astype(jnp.bfloat16)
            to_f.start()
            second.wait_recv()
            bwd[k, SECOND, :] = (
                bwd[k, SECOND, :].astype(jnp.float32) + half_b[k].astype(jnp.float32)
            ).astype(jnp.bfloat16)
            to_b.start()

        @pl.when(i >= 2)
        def _():
            k = i - 2
            from_b, from_f = full_copies(k)
            from_b.wait_recv()
            from_f.wait_recv()
            total = mine[k] + got_f[k].astype(jnp.float32) + got_b[k].astype(jnp.float32)
            done[k] = (state[:, cols(k)].astype(jnp.float32) + total).astype(jnp.bfloat16)
            shift_copy(k).start()

        return carry

    lax.fori_loop(0, NJ + 2, step, 0)

    for copy in sent:
        copy.wait_send()
    for dy in range(YS):
        att_copy(dy).wait_send()

    def finish(k, carry):
        for copy in half_copies(k) + full_copies(k):
            copy.wait_send()
        shift_copy(k).wait()
        return carry

    lax.fori_loop(0, NJ, finish, 0)
    remote(docs_ref, odocs_ref, dsend.at[9], drecv.at[9], following).wait_recv()


def local(state, docs, gain, w_query, w_keyval, w_out):
    width = state.shape[2]
    cw = width // NJ
    bf, f32 = jnp.bfloat16, jnp.float32
    dma = pltpu.SemaphoreType.DMA
    anyspace = pl.BlockSpec(memory_space=pl.ANY)
    return tuple(pl.pallas_call(
        body,
        out_shape=(
            jax.ShapeDtypeStruct(state.shape, state.dtype),
            jax.ShapeDtypeStruct(docs.shape, docs.dtype),
        ),
        in_specs=[anyspace] * 6,
        out_specs=(anyspace, anyspace),
        scratch_shapes=[
            pltpu.VMEM((BLK, width), bf),
            pltpu.VMEM((1, width), f32),
            pltpu.VMEM((8, BLK, width), bf),
            pltpu.VMEM((3, width, 2 * HD), bf),
            pltpu.VMEM((2, 4 * HD, width), bf),
            pltpu.VMEM((8, 4, BLK, HD), bf),
            pltpu.VMEM((16 + PAD, BLK, 2 * HD), bf),
            pltpu.VMEM((16 + PAD, 1, BLK), jnp.int32),
            pltpu.VMEM((2, YS, BLK, 4 * HD), bf),
            pltpu.VMEM((YS, BLK, 4 * HD), bf),
            pltpu.VMEM((NJ, BLK, cw), bf),
            pltpu.VMEM((NJ, BLK, cw), bf),
            pltpu.VMEM((NJ, BLK, cw), bf),
            pltpu.VMEM((NJ, BLK, cw), f32),
            pltpu.VMEM((NJ, HALF, cw), bf),
            pltpu.VMEM((NJ, HALF, cw), bf),
            pltpu.VMEM((NJ, BLK, cw), bf),
            pltpu.VMEM((NJ, BLK, cw), bf),
            pltpu.VMEM((NJ, BLK, cw), bf),
            dma((6,)),
            dma((14,)), dma((8, 2)),
            dma((10,)), dma((10,)),
            dma((2,)), dma((2,)),
            dma((8,)), dma((8,)),
            dma((2 * NW + 1,)), dma((2 * NW + 1,)),
            dma((YS,)), dma((YS,)),
            dma((4, NJ)), dma((4, NJ)),
            dma((NJ,)), dma((NJ,)),
        ],
        compiler_params=pltpu.CompilerParams(
            collective_id=0, has_side_effects=True, vmem_limit_bytes=60 << 20
        ),
        name="layer",
    )(state, docs, gain, w_query, w_keyval, w_out))


def solution(mesh):
    in_specs = (
        P("section", "tensor", None),
        P("section", "tensor"),
        P("section", None),
        P("section", None, "tensor"),
        P("section", None, "tensor"),
        P("section", "tensor", None),
    )
    out_specs = (P("section", "tensor", None), P("section", "tensor"))
    return jax.shard_map(local, mesh=mesh, in_specs=in_specs, out_specs=out_specs, check_vma=False)
```

time: 439 us -> 171 us (0.39)
  waiting for transfers between devices: 302 us -> 0 us
  Pallas kernels: 0 us -> 167 us
  matrix products: 68.8 us -> 0 us
  blocking collectives: 24.4 us -> 0 us
  between operations: 14.1 us -> 0.65 us
  other arithmetic: 13.4 us -> 0 us
  local copies, waits for them, and re-layouts: 8.47 us -> 2.97 us
    pallas_call x0 -> x1, Pallas kernels: none -> 167 us  [local(): pl.pallas_call(body, out_shape=(jax.ShapeDtypeStruct(state.shape, state.d...]
    reduce_scatter x1 -> x0, waiting for transfers between devices: 166 us -> none  [local(): lax.psum_scatter(jnp.dot(attended, w_out[0], preferred_element_type=jnp.f...]
    all_gather x1 -> x0, waiting for transfers between devices: 106 us -> none  [local(): lax.all_gather(normed, 'tensor', axis=0, tiled=True)]
    dot_general x19 -> x0, matrix products: 68.8 us -> none  [the longest x8 18.8 us: attend(): jnp.dot(query_rows, key_rows.T, preferred_element_type=jnp.float32)]
    ppermute x3 -> x0, waiting for transfers between devices: 29.1 us -> none  [the longest x2 29.1 us: shifted(): lax.ppermute(value, axis, [(i, (i + by) % size) for i in range(size)])]
    all_gather x1 -> x0, blocking collectives: 24.4 us -> none  [local(): lax.all_gather(docs[0], 'tensor', axis=0, tiled=True)]
    reduce_sum x9 -> x0, other arithmetic: 7.49 us -> none  [the longest x8 5.69 us: attend(): probs = (expo / jnp.sum(expo, axis=-1, keepdims=True)).astype(jnp.bfloat16)]
  transfers between devices with their start and end apart: 5 -> 0, of which waited for: 3 -> 0; matrix products, arithmetic and copies ran while one was open for 2% -> 0% of each run, Pallas kernels for 0% -> 0%
where the time goes in v1:
time: 171 us
  Pallas kernels  167 us (98%)
  local copies, waits for them, and re-layouts  2.97 us (2%)
    pallas_call x1, Pallas kernels, local(): pl.pallas_call(body, out_shape=(jax.ShapeDtypeStruct(state.shape, state.d...  167 us

profile of v1, /device:TPU:0, one launch (start us, length us, event | category | flops | bytes accessed | tf_op | source)
XLA Modules:
  0.0 170.8 jit_solution(13973024798693118493)
XLA Ops:
  0.6 167.2 %layer.1 = (bf16[1,128,5120]{2,1,0:T(8,128)(2,1)}, s32[1,128]{1,0:T(1,128)}) custom-call(bf16[1,128,5120]{2,1,0:T(8,128)(2,1)} %state_ref.1, s32[1,128]{1,0:T(1,128)} %docs_ref.1, f32[1,5120]{1,0:T(1,128)} %gain_ref.1, bf16[1,5120,256]{2,1,0:T(8,128)(2,1)} %wq_ref.1, bf16[1,5120,128]{2,1,0:T(8,128)(2,1)} %wkv_ref.1, bf16[1,256,5120]{2,1,0:T(8,128)(2,1)} %wo_ref.1), custom_call_target="tpu_custom_call" | custom-call | tf_op jit(solution)/shard_map/layer/pallas_call | solution.py:384
  167.9 0.0 copy-start
  167.9 2.5 %copy.10 = bf16[1,128,5120]{2,1,0:T(8,128)(2,1)} copy(bf16[1,128,5120]{2,1,0:T(8,128)(2,1)} %get-tuple-element.4) | data formatting | bytes 2621440
  170.3 0.0 copy-done
  170.3 0.5 copy.11
Async XLA Ops:
  167.9 2.5 %copy-start = (s32[1,128]{1,0:T(1,128)S(1)}, s32[1,128]{1,0:T(1,128)}, u32[]{:S(2)}) copy-start(s32[1,128]{1,0:T(1,128)} %get-tuple-element.5) | copy-start | bytes 1540

commit v2 on v1

--- a/solution.py
+++ b/solution.py
@@ -15,6 +15,7 @@
 PAD = WIN - 1
 YS = 4
 NJ = 10
+LAG = 3
 NW = 5
 SLOTS = ((0, 0), (1, 0), (0, 3), (0, 1), (1, 3), (1, 1), (0, 2), (1, 2))
 OWN, ACROSS, BEHIND, AHEAD, BEHIND2, AHEAD2, FAR, FAR2 = range(8)
@@ -26,8 +27,8 @@
 def body(
     state_ref, docs_ref, gain_ref, wq_ref, wkv_ref, wo_ref,
     out_ref, odocs_ref,
-    state, gain, xg, w, wo, q, kv, dc, att, att_out,
-    far, fwd, bwd, mine, half_f, half_b, got_f, got_b, done,
+    state, gain, xg, w, wo, q, kv, dc, att,
+    far, fwd, bwd, half_f, half_b, got_f, got_b, done,
     load_sem, xs_sem, xr_sem, dsend, drecv, ws_sem, wr_sem, kvs_sem, kvr_sem,
     wos_sem, wor_sem, ats_sem, atr_sem, rs_send, rs_recv, sh_send, sh_recv,
 ):
@@ -118,13 +119,12 @@
     norm(FIRST)
     pl.semaphore_wait(barrier, 6)
     go(piece(0, OWN, BEHIND, 0, ahead))
-    go(piece(1, OWN, ACROSS, 0, across))
+    across_first = piece(1, OWN, ACROSS, 0, across)
+    across_first.start()
     norm(SECOND)
     go(piece(2, OWN, AHEAD, 1, behind))
     go(piece(3, OWN, BEHIND, 1, ahead))
     go(piece(4, OWN, AHEAD, 0, behind))
-    across_last = piece(5, OWN, ACROSS, 1, across)
-    across_last.start()
 
     loads[2].wait()
     own_docs = dc.at[PAD + 2 * block_of(0, 0) + core]
@@ -141,7 +141,7 @@
 
     def project(slot, count):
         rows = xg[pl.ds(slot, count)].reshape(count * BLK, width)
-        for index in range(3):
+        for index in (2, 0, 1):
             res = jnp.dot(rows, w[index], preferred_element_type=jnp.float32).astype(jnp.bfloat16)
             for one in range(count):
                 dh, dy = SLOTS[slot + one]
@@ -150,11 +150,9 @@
                     q[dh * YS + dy, 2 * index] = part[:, :HD]
                     q[dh * YS + dy, 2 * index + 1] = part[:, HD:]
                 else:
-                    kv[PAD + 2 * block_of(dh, dy) + core] = part
-        for one in range(count):
-            dh, dy = SLOTS[slot + one]
-            ref = kv.at[PAD + 2 * block_of(dh, dy) + core]
-            go(remote(ref, ref, kvs_sem.at[slot + one], kvr_sem.at[slot + one], twin))
+                    ref = kv.at[PAD + 2 * block_of(dh, dy) + core]
+                    ref[...] = part
+                    go(remote(ref, ref, kvs_sem.at[slot + one], kvr_sem.at[slot + one], twin))
 
     def wo_piece(chunk):
         return pl.ds(chunk * ww, ww)
@@ -171,19 +169,22 @@
         wo_across(chunk).wait_recv()
         go(wo_relay(chunk))
 
+    across_first.wait_send()
+    across_last = piece(5, OWN, ACROSS, 1, across)
+    across_last.start()
+    arrived(ACROSS, 0)
+    go(piece(8, ACROSS, BEHIND2, 0, ahead))
+    go(piece(10, ACROSS, AHEAD2, 0, behind))
     arrived(BEHIND, 0)
     go(piece(6, BEHIND, FAR, 0, ahead))
     arrived(AHEAD, 1)
     go(piece(7, AHEAD, FAR, 1, behind))
-    arrived(ACROSS, 0)
-    go(piece(8, ACROSS, BEHIND2, 0, ahead))
-    go(piece(10, ACROSS, AHEAD2, 0, behind))
-    across_last.wait_send()
-    for chunk in range(NW):
-        go(wo_across(chunk))
     arrived(ACROSS, 1)
     go(piece(9, ACROSS, AHEAD2, 1, behind))
     go(piece(11, ACROSS, BEHIND2, 1, ahead))
+    across_last.wait_send()
+    for chunk in range(3):
+        go(wo_across(chunk))
     docs_arrived(1, 1, 0)
     go(send_docs(4, 1, 0, 4, ahead))
     go(send_docs(5, 1, 0, 5, behind))
@@ -207,24 +208,26 @@
     arrived(BEHIND, 1)
     arrived(AHEAD, 0)
     project(BEHIND, 2)
-    pass_wo(0)
+    go(wo_across(3))
     arrived(BEHIND2, 0)
     go(piece(12, BEHIND2, FAR2, 0, ahead))
     arrived(AHEAD2, 1)
     go(piece(13, AHEAD2, FAR2, 1, behind))
-    pass_wo(1)
     arrived(FAR, 0)
     arrived(FAR, 1)
     project(FAR, 1)
-    pass_wo(2)
+    go(wo_across(4))
+    pass_wo(0)
     arrived(BEHIND2, 1)
     arrived(AHEAD2, 0)
     project(BEHIND2, 2)
+    pass_wo(1)
     docs_arrived(6, 0, 2)
     docs_arrived(7, 1, 2)
     arrived(FAR2, 0)
     arrived(FAR2, 1)
     project(FAR2, 1)
+    pass_wo(2)
     pass_wo(3)
     for slot in range(8):
         dh, dy = SLOTS[slot]
@@ -264,30 +267,33 @@
         ).reshape(4, BLK, HD)
         return (res / total).astype(jnp.bfloat16)
 
-    def att_copy(dy):
-        return remote(att_out.at[dy], att.at[1, dy], ats_sem.at[dy], atr_sem.at[dy], across)
-
-    def attend_other(dy, carry):
-        res = attend(1, dy)
-        for head in range(4):
-            att_out[dy, :, head * HD : (head + 1) * HD] = res[head]
-        att_copy(dy).start()
-        return carry
-
-    def attend_own(dy, carry):
-        res = attend(0, dy)
-        for head in range(4):
-            att[0, dy, :, head * HD : (head + 1) * HD] = res[head]
-        return carry
-
-    lax.fori_loop(0, YS, attend_other, 0)
+    def att_copy(place):
+        return remote(att.at[2, place], att.at[1, place], ats_sem.at[place], atr_sem.at[place], across)
+
+    def attend_all(order):
+        def one(i, carry):
+            code = jnp.int32(order[-1])
+            for index in range(len(order) - 1):
+                code = jnp.where(i == index, order[index], code)
+            dh, place = code // YS, code % YS
+            dy = jnp.where(place < 2, 2 - place, 9 - 3 * place)
+            res = attend(dh, dy)
+            for head in range(4):
+                att[2 * dh, place, :, head * HD : (head + 1) * HD] = res[head]
+
+            @pl.when(dh == 1)
+            def _():
+                att_copy(place).start()
+
+            return carry
+
+        lax.fori_loop(0, len(order), one, 0)
+
+    attend_all((4, 0, 1, 5, 6))
     pass_wo(4)
-    lax.fori_loop(0, YS, attend_own, 0)
-
     own_wo = wo.at[0, pl.ds(pl.multiple_of((1 - core) * 256, 256), 256), :]
     remote(own_wo, own_wo, wos_sem.at[2 * NW], wor_sem.at[2 * NW], twin).wait_recv()
-    for dy in range(YS):
-        att_copy(dy).wait_recv()
+    att_copy(0).wait_recv()
 
     def half_copies(k):
         return (
@@ -307,7 +313,17 @@
     def shift_copy(k):
         return remote(done.at[k], out_ref.at[0, :, cols(k)], sh_send.at[k], sh_recv.at[k], following)
 
-    def step(i, carry):
+    def product(first, count, k):
+        return sum(
+            jnp.dot(
+                att[group, pl.ds(first, count)].reshape(count * BLK, 4 * HD),
+                wo[group, :, cols(k)],
+                preferred_element_type=jnp.float32,
+            )
+            for group in range(2)
+        )
+
+    def far_step(i, carry):
         for chunk in range(NW):
             @pl.when(i == chunk * (NJ // NW))
             def _():
@@ -316,54 +332,54 @@
                     ref, ref, wos_sem.at[NW + chunk], wor_sem.at[NW + chunk], twin
                 ).wait_recv()
 
+        far[i] = product(0, 1, i).astype(jnp.bfloat16)
+        for copy in half_copies(i):
+            copy.start()
+        return carry
+
+    lax.fori_loop(0, NJ, far_step, 0)
+    attend_all((2, 7, 3))
+    att_copy(1).wait_recv()
+    att_copy(2).wait_recv()
+
+    def step(i, carry):
         @pl.when(i < NJ)
         def _():
-            res = jnp.dot(
-                att[0].reshape(YS * BLK, 4 * HD), wo[0, :, cols(i)], preferred_element_type=jnp.float32
-            ) + jnp.dot(
-                att[1].reshape(YS * BLK, 4 * HD), wo[1, :, cols(i)], preferred_element_type=jnp.float32
-            )
-            far[i] = res[2 * BLK : 3 * BLK].astype(jnp.bfloat16)
-            for copy in half_copies(i):
-                copy.start()
-            mine[i] = res[:BLK]
-            fwd[i] = res[BLK : 2 * BLK].astype(jnp.bfloat16)
-            bwd[i] = res[3 * BLK :].astype(jnp.bfloat16)
-
-        @pl.when((i >= 1) & (i <= NJ))
-        def _():
-            k = i - 1
-            first, second = half_copies(k)
-            to_f, to_b = full_copies(k)
+            res = product(1, 2, i)
+            first, second = half_copies(i)
+            to_f, to_b = full_copies(i)
             first.wait_recv()
-            fwd[k, FIRST, :] = (
-                fwd[k, FIRST, :].astype(jnp.float32) + half_f[k].astype(jnp.float32)
-            ).astype(jnp.bfloat16)
+            fwd[i, SECOND, :] = res[HALF:BLK].astype(jnp.bfloat16)
+            fwd[i, FIRST, :] = (res[:HALF] + half_f[i].astype(jnp.float32)).astype(jnp.bfloat16)
             to_f.start()
             second.wait_recv()
-            bwd[k, SECOND, :] = (
-                bwd[k, SECOND, :].astype(jnp.float32) + half_b[k].astype(jnp.float32)
-            ).astype(jnp.bfloat16)
+            bwd[i, FIRST, :] = res[BLK : BLK + HALF].astype(jnp.bfloat16)
+            bwd[i, SECOND, :] = (res[BLK + HALF :] + half_b[i].astype(jnp.float32)).astype(jnp.bfloat16)
             to_b.start()
 
-        @pl.when(i >= 2)
+        @pl.when(i == LAG)
         def _():
-            k = i - 2
+            att_copy(3).wait_recv()
+
+        @pl.when(i >= LAG)
+        def _():
+            k = i - LAG
+            total = state[:, cols(k)].astype(jnp.float32) + product(3, 1, k)
             from_b, from_f = full_copies(k)
             from_b.wait_recv()
             from_f.wait_recv()
-            total = mine[k] + got_f[k].astype(jnp.float32) + got_b[k].astype(jnp.float32)
-            done[k] = (state[:, cols(k)].astype(jnp.float32) + total).astype(jnp.bfloat16)
+            total = total + got_f[k].astype(jnp.float32) + got_b[k].astype(jnp.float32)
+            done[k] = total.astype(jnp.bfloat16)
             shift_copy(k).start()
 
         return carry
 
-    lax.fori_loop(0, NJ + 2, step, 0)
+    lax.fori_loop(0, NJ + LAG, step, 0)
 
     for copy in sent:
         copy.wait_send()
-    for dy in range(YS):
-        att_copy(dy).wait_send()
+    for place in range(YS):
+        att_copy(place).wait_send()
 
     def finish(k, carry):
         for copy in half_copies(k) + full_copies(k):
@@ -398,12 +414,10 @@
             pltpu.VMEM((8, 4, BLK, HD), bf),
             pltpu.VMEM((16 + PAD, BLK, 2 * HD), bf),
             pltpu.VMEM((16 + PAD, 1, BLK), jnp.int32),
-            pltpu.VMEM((2, YS, BLK, 4 * HD), bf),
-            pltpu.VMEM((YS, BLK, 4 * HD), bf),
-            pltpu.VMEM((NJ, BLK, cw), bf),
-            pltpu.VMEM((NJ, BLK, cw), bf),
-            pltpu.VMEM((NJ, BLK, cw), bf),
-            pltpu.VMEM((NJ, BLK, cw), f32),
+            pltpu.VMEM((3, YS, BLK, 4 * HD), bf),
+            pltpu.VMEM((NJ, BLK, cw), bf),
+            pltpu.VMEM((NJ, BLK, cw), bf),
+            pltpu.VMEM((NJ, BLK, cw), bf),
             pltpu.VMEM((NJ, HALF, cw), bf),
             pltpu.VMEM((NJ, HALF, cw), bf),
             pltpu.VMEM((NJ, BLK, cw), bf),

time: 171 us -> 164 us (0.959)
  Pallas kernels: 167 us -> 160 us
    pallas_call x1, Pallas kernels: 167 us -> 160 us  [local(): pl.pallas_call(body, out_shape=(jax.ShapeDtypeStruct(state.shape, state.d...]
where the time goes in v2:
time: 164 us
  Pallas kernels  160 us (98%)
  local copies, waits for them, and re-layouts  2.97 us (2%)
    pallas_call x1, Pallas kernels, local(): pl.pallas_call(body, out_shape=(jax.ShapeDtypeStruct(state.shape, state.d...  160 us

profile of v2, /device:TPU:0, one launch (start us, length us, event | category | flops | bytes accessed | tf_op | source)
XLA Modules:
  0.0 163.9 jit_solution(7865983938776669016)
XLA Ops:
  0.6 160.3 %layer.1 = (bf16[1,128,5120]{2,1,0:T(8,128)(2,1)}, s32[1,128]{1,0:T(1,128)}) custom-call(bf16[1,128,5120]{2,1,0:T(8,128)(2,1)} %state_ref.1, s32[1,128]{1,0:T(1,128)} %docs_ref.1, f32[1,5120]{1,0:T(1,128)} %gain_ref.1, bf16[1,5120,256]{2,1,0:T(8,128)(2,1)} %wq_ref.1, bf16[1,5120,128]{2,1,0:T(8,128)(2,1)} %wkv_ref.1, bf16[1,256,5120]{2,1,0:T(8,128)(2,1)} %wo_ref.1), custom_call_target="tpu_custom_call" | custom-call | tf_op jit(solution)/shard_map/layer/pallas_call | solution.py:400
  160.9 0.0 copy-start
  160.9 2.5 %copy.10 = bf16[1,128,5120]{2,1,0:T(8,128)(2,1)} copy(bf16[1,128,5120]{2,1,0:T(8,128)(2,1)} %get-tuple-element.4) | data formatting | bytes 2621440
  163.4 0.0 copy-done
  163.4 0.5 copy.11
Async XLA Ops:
  160.9 2.5 %copy-start = (s32[1,128]{1,0:T(1,128)S(1)}, s32[1,128]{1,0:T(1,128)}, u32[]{:S(2)}) copy-start(s32[1,128]{1,0:T(1,128)} %get-tuple-element.5) | copy-start | bytes 1540

commit v3 on v2

--- a/solution.py
+++ b/solution.py
@@ -14,8 +14,8 @@
 WIN = 5
 PAD = WIN - 1
 YS = 4
-NJ = 10
-LAG = 3
+NJ = 20
+LAG = 7
 NW = 5
 SLOTS = ((0, 0), (1, 0), (0, 3), (0, 1), (1, 3), (1, 1), (0, 2), (1, 2))
 OWN, ACROSS, BEHIND, AHEAD, BEHIND2, AHEAD2, FAR, FAR2 = range(8)
@@ -175,13 +175,10 @@
     arrived(ACROSS, 0)
     go(piece(8, ACROSS, BEHIND2, 0, ahead))
     go(piece(10, ACROSS, AHEAD2, 0, behind))
-    arrived(BEHIND, 0)
-    go(piece(6, BEHIND, FAR, 0, ahead))
-    arrived(AHEAD, 1)
-    go(piece(7, AHEAD, FAR, 1, behind))
     arrived(ACROSS, 1)
     go(piece(9, ACROSS, AHEAD2, 1, behind))
-    go(piece(11, ACROSS, BEHIND2, 1, ahead))
+    last_ahead = piece(11, ACROSS, BEHIND2, 1, ahead)
+    last_ahead.start()
     across_last.wait_send()
     for chunk in range(3):
         go(wo_across(chunk))
@@ -205,34 +202,11 @@
     docs_arrived(4, 1, 3)
     go(send_docs(7, 1, 3, 7, ahead))
     docs_arrived(5, 1, 1)
-    arrived(BEHIND, 1)
-    arrived(AHEAD, 0)
-    project(BEHIND, 2)
-    go(wo_across(3))
-    arrived(BEHIND2, 0)
-    go(piece(12, BEHIND2, FAR2, 0, ahead))
-    arrived(AHEAD2, 1)
-    go(piece(13, AHEAD2, FAR2, 1, behind))
-    arrived(FAR, 0)
-    arrived(FAR, 1)
-    project(FAR, 1)
-    go(wo_across(4))
-    pass_wo(0)
-    arrived(BEHIND2, 1)
-    arrived(AHEAD2, 0)
-    project(BEHIND2, 2)
-    pass_wo(1)
-    docs_arrived(6, 0, 2)
-    docs_arrived(7, 1, 2)
-    arrived(FAR2, 0)
-    arrived(FAR2, 1)
-    project(FAR2, 1)
-    pass_wo(2)
-    pass_wo(3)
-    for slot in range(8):
-        dh, dy = SLOTS[slot]
-        ref = kv.at[PAD + 2 * block_of(dh, dy) + 1 - core]
-        remote(ref, ref, kvs_sem.at[slot], kvr_sem.at[slot], twin).wait_recv()
+    def twin_keys(slots):
+        for slot in slots:
+            dh, dy = SLOTS[slot]
+            ref = kv.at[PAD + 2 * block_of(dh, dy) + 1 - core]
+            remote(ref, ref, kvs_sem.at[slot], kvr_sem.at[slot], twin).wait_recv()
 
     factor = HD ** (-0.5) * LOG2E
 
@@ -289,7 +263,38 @@
 
         lax.fori_loop(0, len(order), one, 0)
 
-    attend_all((4, 0, 1, 5, 6))
+    for slot in (BEHIND, AHEAD):
+        for part in range(2):
+            arrived(slot, part)
+    project(BEHIND, 2)
+    go(wo_across(3))
+    arrived(BEHIND2, 0)
+    go(piece(12, BEHIND2, FAR2, 0, ahead))
+    arrived(AHEAD2, 1)
+    go(piece(13, AHEAD2, FAR2, 1, behind))
+    last_ahead.wait_send()
+    go(piece(6, BEHIND, FAR, 0, ahead))
+    go(piece(7, AHEAD, FAR, 1, behind))
+    go(wo_across(4))
+    pass_wo(0)
+    arrived(BEHIND2, 1)
+    arrived(AHEAD2, 0)
+    project(BEHIND2, 2)
+    pass_wo(1)
+    docs_arrived(6, 0, 2)
+    docs_arrived(7, 1, 2)
+    arrived(FAR2, 0)
+    arrived(FAR2, 1)
+    project(FAR2, 1)
+    twin_keys((OWN, ACROSS, BEHIND, AHEAD, BEHIND2, AHEAD2, FAR2))
+    attend_all((4, 5, 1))
+    pass_wo(2)
+    pass_wo(3)
+    arrived(FAR, 0)
+    arrived(FAR, 1)
+    project(FAR, 1)
+    twin_keys((FAR,))
+    attend_all((0, 6))
     pass_wo(4)
     own_wo = wo.at[0, pl.ds(pl.multiple_of((1 - core) * 256, 256), 256), :]
     remote(own_wo, own_wo, wos_sem.at[2 * NW], wor_sem.at[2 * NW], twin).wait_recv()
@@ -338,7 +343,7 @@
         return carry
 
     lax.fori_loop(0, NJ, far_step, 0)
-    attend_all((2, 7, 3))
+    attend_all((7, 2, 3))
     att_copy(1).wait_recv()
     att_copy(2).wait_recv()
 

time: 164 us -> 158 us (0.963)
  Pallas kernels: 160 us -> 153 us
    pallas_call x1, Pallas kernels: 160 us -> 153 us  [local(): pl.pallas_call(body, out_shape=(jax.ShapeDtypeStruct(state.shape, state.d...]
where the time goes in v3:
time: 158 us; the launch traced here: 157 us
  Pallas kernels  153 us (97%)
  local copies, waits for them, and re-layouts  2.97 us (2%)
    pallas_call x1, Pallas kernels, local(): pl.pallas_call(body, out_shape=(jax.ShapeDtypeStruct(state.shape, state.d...  153 us

profile of v3, /device:TPU:0, one launch (start us, length us, event | category | flops | bytes accessed | tf_op | source)
XLA Modules:
  0.0 157.0 jit_solution(3350852193656096651)
XLA Ops:
  0.6 153.4 %layer.1 = (bf16[1,128,5120]{2,1,0:T(8,128)(2,1)}, s32[1,128]{1,0:T(1,128)}) custom-call(bf16[1,128,5120]{2,1,0:T(8,128)(2,1)} %state_ref.1, s32[1,128]{1,0:T(1,128)} %docs_ref.1, f32[1,5120]{1,0:T(1,128)} %gain_ref.1, bf16[1,5120,256]{2,1,0:T(8,128)(2,1)} %wq_ref.1, bf16[1,5120,128]{2,1,0:T(8,128)(2,1)} %wkv_ref.1, bf16[1,256,5120]{2,1,0:T(8,128)(2,1)} %wo_ref.1), custom_call_target="tpu_custom_call" | custom-call | tf_op jit(solution)/shard_map/layer/pallas_call | solution.py:405
  154.1 0.0 copy-start
  154.1 2.5 %copy.10 = bf16[1,128,5120]{2,1,0:T(8,128)(2,1)} copy(bf16[1,128,5120]{2,1,0:T(8,128)(2,1)} %get-tuple-element.4) | data formatting | bytes 2621440
  156.5 0.0 copy-done
  156.5 0.5 copy.11
Async XLA Ops:
  154.1 2.5 %copy-start = (s32[1,128]{1,0:T(1,128)S(1)}, s32[1,128]{1,0:T(1,128)}, u32[]{:S(2)}) copy-start(s32[1,128]{1,0:T(1,128)} %get-tuple-element.5) | copy-start | bytes 1540

commit v4 on v3

--- a/solution.py
+++ b/solution.py
@@ -266,7 +266,6 @@
     for slot in (BEHIND, AHEAD):
         for part in range(2):
             arrived(slot, part)
-    project(BEHIND, 2)
     go(wo_across(3))
     arrived(BEHIND2, 0)
     go(piece(12, BEHIND2, FAR2, 0, ahead))
@@ -276,6 +275,7 @@
     go(piece(6, BEHIND, FAR, 0, ahead))
     go(piece(7, AHEAD, FAR, 1, behind))
     go(wo_across(4))
+    project(BEHIND, 2)
     pass_wo(0)
     arrived(BEHIND2, 1)
     arrived(AHEAD2, 0)
@@ -294,7 +294,7 @@
     arrived(FAR, 1)
     project(FAR, 1)
     twin_keys((FAR,))
-    attend_all((0, 6))
+    attend_all((0,))
     pass_wo(4)
     own_wo = wo.at[0, pl.ds(pl.multiple_of((1 - core) * 256, 256), 256), :]
     remote(own_wo, own_wo, wos_sem.at[2 * NW], wor_sem.at[2 * NW], twin).wait_recv()
@@ -343,7 +343,7 @@
         return carry
 
     lax.fori_loop(0, NJ, far_step, 0)
-    attend_all((7, 2, 3))
+    attend_all((6, 7, 2, 3))
     att_copy(1).wait_recv()
     att_copy(2).wait_recv()
 
@@ -439,7 +439,7 @@
             dma((NJ,)), dma((NJ,)),
         ],
         compiler_params=pltpu.CompilerParams(
-            collective_id=0, has_side_effects=True, vmem_limit_bytes=60 << 20
+            collective_id=0, has_side_effects=True, vmem_limit_bytes=52 << 20
         ),
         name="layer",
     )(state, docs, gain, w_query, w_keyval, w_out))

time: 158 us -> 153 us (0.968)
  Pallas kernels: 153 us -> 150 us
    pallas_call x1, Pallas kernels: 153 us -> 150 us  [local(): pl.pallas_call(body, out_shape=(jax.ShapeDtypeStruct(state.shape, state.d...]
where the time goes in v4:
time: 153 us
  Pallas kernels  150 us (98%)
  local copies, waits for them, and re-layouts  2.94 us (2%)
    pallas_call x1, Pallas kernels, local(): pl.pallas_call(body, out_shape=(jax.ShapeDtypeStruct(state.shape, state.d...  150 us

profile of v4, /device:TPU:0, one launch (start us, length us, event | category | flops | bytes accessed | tf_op | source)
XLA Modules:
  0.0 153.3 jit_solution(11679444466981815573)
XLA Ops:
  0.6 0.0 copy-start
  0.6 0.7 copy-done
  1.4 0.0 copy-start.1
  1.4 0.7 copy-done.1
  2.0 149.7 %layer.1 = (bf16[1,128,5120]{2,1,0:T(8,128)(2,1)S(1)}, s32[1,128]{1,0:T(1,128)S(1)}) custom-call(bf16[1,128,5120]{2,1,0:T(8,128)(2,1)} %state_ref.1, s32[1,128]{1,0:T(1,128)S(1)} %copy-done.1, f32[1,5120]{1,0:T(1,128)S(1)} %copy-done, bf16[1,5120,256]{2,1,0:T(8,128)(2,1)} %wq_ref.1, bf16[1,5120,128]{2,1,0:T(8,128)(2,1)} %wkv_ref.1, bf16[1,256,5120]{2,1,0:T(8,128)(2,1)} %wo_ref.1), custom_call_target="tpu_custom_call" | custom-call | tf_op jit(solution)/shard_map/layer/pallas_call | solution.py:405
  151.7 1.1 copy.10
  152.8 0.5 copy.11
Async XLA Ops:
  0.6 0.7 copy-start
  1.4 0.7 copy-start.1

commit v5 on v4

--- a/solution.py
+++ b/solution.py
@@ -15,6 +15,7 @@
 PAD = WIN - 1
 YS = 4
 NJ = 20
+EARLY = 6
 LAG = 7
 NW = 5
 SLOTS = ((0, 0), (1, 0), (0, 3), (0, 1), (1, 3), (1, 1), (0, 2), (1, 2))
@@ -342,8 +343,10 @@
             copy.start()
         return carry
 
-    lax.fori_loop(0, NJ, far_step, 0)
-    attend_all((6, 7, 2, 3))
+    lax.fori_loop(0, EARLY, far_step, 0)
+    attend_all((6, 7))
+    lax.fori_loop(EARLY, NJ, far_step, 0)
+    attend_all((2, 3))
     att_copy(1).wait_recv()
     att_copy(2).wait_recv()
 

time: 153 us -> 153 us (level)
  no operation moved by 1% of the time
where the time goes in v5:
time: 153 us
  Pallas kernels  150 us (98%)
  local copies, waits for them, and re-layouts  2.94 us (2%)
    pallas_call x1, Pallas kernels, local(): pl.pallas_call(body, out_shape=(jax.ShapeDtypeStruct(state.shape, state.d...  150 us

profile of v5, /device:TPU:0, one launch (start us, length us, event | category | flops | bytes accessed | tf_op | source)
XLA Modules:
  0.0 153.3 jit_solution(3441765512441776774)
XLA Ops:
  0.6 0.0 copy-start
  0.6 0.7 copy-done
  1.4 0.0 copy-start.1
  1.4 0.7 copy-done.1
  2.0 149.7 %layer.1 = (bf16[1,128,5120]{2,1,0:T(8,128)(2,1)S(1)}, s32[1,128]{1,0:T(1,128)S(1)}) custom-call(bf16[1,128,5120]{2,1,0:T(8,128)(2,1)} %state_ref.1, s32[1,128]{1,0:T(1,128)S(1)} %copy-done.1, f32[1,5120]{1,0:T(1,128)S(1)} %copy-done, bf16[1,5120,256]{2,1,0:T(8,128)(2,1)} %wq_ref.1, bf16[1,5120,128]{2,1,0:T(8,128)(2,1)} %wkv_ref.1, bf16[1,256,5120]{2,1,0:T(8,128)(2,1)} %wo_ref.1), custom_call_target="tpu_custom_call" | custom-call | tf_op jit(solution)/shard_map/layer/pallas_call | solution.py:408
  151.7 1.1 copy.10
  152.8 0.5 copy.11
Async XLA Ops:
  0.6 0.7 copy-start
  1.4 0.7 copy-start.1

commit v6 on v4

--- a/solution.py
+++ b/solution.py
@@ -119,12 +119,12 @@
     norm(FIRST)
     pl.semaphore_wait(barrier, 6)
     go(piece(0, OWN, BEHIND, 0, ahead))
+    go(piece(4, OWN, AHEAD, 0, behind))
     across_first = piece(1, OWN, ACROSS, 0, across)
     across_first.start()
     norm(SECOND)
     go(piece(2, OWN, AHEAD, 1, behind))
     go(piece(3, OWN, BEHIND, 1, ahead))
-    go(piece(4, OWN, AHEAD, 0, behind))
 
     loads[2].wait()
     own_docs = dc.at[PAD + 2 * block_of(0, 0) + core]

time: 153 us -> 153 us (level)
  no operation moved by 1% of the time
where the time goes in v6:
time: 153 us
  Pallas kernels  150 us (98%)
  local copies, waits for them, and re-layouts  2.94 us (2%)
    pallas_call x1, Pallas kernels, local(): pl.pallas_call(body, out_shape=(jax.ShapeDtypeStruct(state.shape, state.d...  150 us

profile of v6, /device:TPU:0, one launch (start us, length us, event | category | flops | bytes accessed | tf_op | source)
XLA Modules:
  0.0 153.3 jit_solution(7604886122995971072)
XLA Ops:
  0.6 0.0 copy-start
  0.6 0.7 copy-done
  1.4 0.0 copy-start.1
  1.4 0.7 copy-done.1
  2.0 149.7 %layer.1 = (bf16[1,128,5120]{2,1,0:T(8,128)(2,1)S(1)}, s32[1,128]{1,0:T(1,128)S(1)}) custom-call(bf16[1,128,5120]{2,1,0:T(8,128)(2,1)} %state_ref.1, s32[1,128]{1,0:T(1,128)S(1)} %copy-done.1, f32[1,5120]{1,0:T(1,128)S(1)} %copy-done, bf16[1,5120,256]{2,1,0:T(8,128)(2,1)} %wq_ref.1, bf16[1,5120,128]{2,1,0:T(8,128)(2,1)} %wkv_ref.1, bf16[1,256,5120]{2,1,0:T(8,128)(2,1)} %wo_ref.1), custom_call_target="tpu_custom_call" | custom-call | tf_op jit(solution)/shard_map/layer/pallas_call | solution.py:405
  151.7 1.1 copy.10
  152.8 0.5 copy.11
Async XLA Ops:
  0.6 0.7 copy-start
  1.4 0.7 copy-start.1
